TPU v7x, 128 devices: a whole 4x4x4 slice. The times are simulated.
128 devices in a mesh: grp: 4 (over x), ctx: 16 (over y, z_lo, core), tp: 2 (over z_hi).
Axes of the slice: x: 4, y: 4, z: 4 (z_hi: 2, z_lo: 2; z = z_hi * 2 + z_lo), core: 2. Of those that a mesh axis runs over, the one named last changes fastest.
Arguments:
- trunk_out: bfloat16 [2048, 4096], P('ctx', ('grp', 'tp')), may hold values from -6 to 6
- norm_gain: bfloat16 [4, 4096], P('grp', 'ctx'), may hold values from 0.099609375 to 1.8984375
- w_query: bfloat16 [4, 4096, 4096], P('grp', 'ctx', 'tp'), may hold values from -2.34375 to 2.34375
- w_key: bfloat16 [4, 4096, 512], P('grp', 'ctx', 'tp'), may hold values from -0.078125 to 0.078125
- value_weight: bfloat16 [4, 4096, 512], P('grp', 'ctx', 'tp'), may hold values from -0.09375 to 0.09375
- context_gradient: bfloat16 [4, 2048, 4096], P('grp', 'ctx', 'tp'), may hold values from -6 to 6
Outputs:
- trunk_grad: float32 [2048, 4096], P('ctx', ('grp', 'tp'))
All inputs are finite; a program needn't handle non-finite values.
Results may differ from a plain program's by a relative error of at most 0.008.
Values may be sent and summed in bfloat16 or wider, within the bound.
A program may use at most 128 MiB of HBM per device.

v0:
```python
import math

import jax
import jax.numpy as jnp
from jax import lax
from jax.sharding import PartitionSpec as P

QUERY_HEAD_COUNT = 32
KEY_VALUE_HEADS = 4
HEAD_SIZE = 128


EPSILON = 1e-05
MASKED_SCORE = -1e30


def against(left_rows, weight_rows):
    return lax.dot_general(
        left_rows, weight_rows, (((1,), (1,)), ((), ())), preferred_element_type=jnp.float32
    )


def body(trunk_out, norm_gain, w_query, w_key, value_weight, context_gradient):
    row_count = trunk_out.shape[0]
    features = lax.all_gather(trunk_out, ("grp", "tp"), axis=1, tiled=True)
    trunk_f32 = features.astype(jnp.float32)
    inverse = lax.rsqrt(jnp.mean(trunk_f32 * trunk_f32, axis=1, keepdims=True) + EPSILON)
    scaled = trunk_f32 * inverse
    width_q = w_query.shape[2]
    width_kv = w_key.shape[2]
    gain_all, query_all, key_all, value_all = (
        lax.all_gather(norm_gain, "ctx", axis=1, tiled=True),
        lax.all_gather(w_query, "ctx", axis=1, tiled=True),
        lax.all_gather(w_key, "ctx", axis=1, tiled=True),
        lax.all_gather(value_weight, "ctx", axis=1, tiled=True),
    )
    gain_row = gain_all[0].astype(jnp.float32)
    normed = (scaled * gain_row[None, :]).astype(jnp.bfloat16)
    query_sum = jnp.dot(normed, query_all[0], preferred_element_type=jnp.float32)
    key_sum = jnp.dot(normed, key_all[0], preferred_element_type=jnp.float32)
    value_sum = jnp.dot(normed, value_all[0], preferred_element_type=jnp.float32)
    query_rows = query_sum.astype(jnp.bfloat16)
    key_local = key_sum.astype(jnp.bfloat16)
    value_local = value_sum.astype(jnp.bfloat16)
    kv_heads = width_kv // HEAD_SIZE
    per_group_count = QUERY_HEAD_COUNT // KEY_VALUE_HEADS
    keys_all, values_all = (
        lax.all_gather(key_local, "ctx", axis=0, tiled=True),
        lax.all_gather(value_local, "ctx", axis=0, tiled=True),
    )
    total_rows = keys_all.shape[0]
    block_rows = math.gcd(512, total_rows)
    ctx_index = lax.axis_index("ctx")
    first_row = ctx_index * row_count
    block_count = (first_row + row_count + block_rows - 1) // block_rows
    score_scale = HEAD_SIZE ** (-0.5)
    query_heads = query_rows.reshape(row_count, kv_heads, per_group_count, HEAD_SIZE)
    grad_heads = context_gradient[0].reshape(row_count, kv_heads, per_group_count, HEAD_SIZE)
    query_pos = first_row + lax.iota(jnp.int32, row_count)

    def block_scores(block_index):
        start_row = block_index * block_rows
        key_block = lax.dynamic_slice_in_dim(keys_all, start_row, block_rows, 0).reshape(
            block_rows, kv_heads, HEAD_SIZE
        )
        value_block = lax.dynamic_slice_in_dim(values_all, start_row, block_rows, 0).reshape(
            block_rows, kv_heads, HEAD_SIZE
        )
        scores = (
            jnp.einsum("tkgd,skd->kgts", query_heads, key_block, preferred_element_type=jnp.float32)
            * score_scale
        )
        key_pos = start_row + lax.iota(jnp.int32, block_rows)
        allowed = key_pos[None, :] <= query_pos[:, None]
        return (jnp.where(allowed, scores, MASKED_SCORE), key_block, value_block, start_row)

    def forward_step(block_index, loop_state):
        running_max, running_sum, context_acc = loop_state
        scores, key_block, value_block, start_row = block_scores(block_index)
        new_max = jnp.maximum(running_max, jnp.max(scores, axis=-1))
        rescale = jnp.exp(running_max - new_max)
        exp_terms = jnp.exp(scores - new_max[..., None])
        new_sum = running_sum * rescale + jnp.sum(exp_terms, axis=-1)
        update = jnp.einsum(
            "kgts,skd->kgtd",
            exp_terms,
            value_block.astype(jnp.float32),
            precision=lax.Precision.HIGHEST,
        )
        return (new_max, new_sum, context_acc * rescale[..., None] + update)

    start_max = jnp.full((kv_heads, per_group_count, row_count), MASKED_SCORE, jnp.float32)
    start_sum = jnp.zeros((kv_heads, per_group_count, row_count), jnp.float32)
    start_context = jnp.zeros((kv_heads, per_group_count, row_count, HEAD_SIZE), jnp.float32)
    running_max, running_sum, context_acc = lax.fori_loop(
        0, block_count, forward_step, (start_max, start_sum, start_context)
    )
    log_total = running_max + jnp.log(running_sum)
    context = context_acc / running_sum[..., None]
    grad_f32 = jnp.transpose(grad_heads, (1, 2, 0, 3)).astype(jnp.float32)
    row_delta = jnp.sum(grad_f32 * context, axis=-1)

    def backward_step(block_index, loop_state):
        query_acc, key_terms, value_terms = loop_state
        scores, key_block, value_block, start_row = block_scores(block_index)
        probs = jnp.exp(scores - log_total[..., None])
        prob_grad = jnp.einsum(
            "tkgd,skd->kgts", grad_heads, value_block, preferred_element_type=jnp.float32
        )
        score_grad = (probs * (prob_grad - row_delta[..., None]) * score_scale).astype(jnp.bfloat16)
        query_acc = query_acc + jnp.einsum(
            "kgts,skd->tkgd", score_grad, key_block, preferred_element_type=jnp.float32
        )
        probs_low = probs.astype(jnp.bfloat16)
        value_part = jnp.einsum(
            "kgts,tkgd->skd", probs_low, grad_heads, preferred_element_type=jnp.float32
        )
        key_part = jnp.einsum(
            "kgts,tkgd->skd", score_grad, query_heads, preferred_element_type=jnp.float32
        )
        key_terms = lax.dynamic_update_slice_in_dim(
            key_terms, key_part.reshape(block_rows, width_kv), start_row, 0
        )
        value_terms = lax.dynamic_update_slice_in_dim(
            value_terms, value_part.reshape(block_rows, width_kv), start_row, 0
        )
        return (query_acc, key_terms, value_terms)

    start_query = jnp.zeros((row_count, kv_heads, per_group_count, HEAD_SIZE), jnp.float32)
    start_terms = jnp.zeros((total_rows, width_kv), jnp.float32)
    query_acc, key_terms, value_terms = lax.fori_loop(
        0, block_count, backward_step, (start_query, start_terms, start_terms)
    )
    query_grad = query_acc.reshape(row_count, width_q).astype(jnp.bfloat16)
    key_own, value_own = (
        lax.psum_scatter(key_terms, "ctx", scatter_dimension=0, tiled=True),
        lax.psum_scatter(value_terms, "ctx", scatter_dimension=0, tiled=True),
    )
    key_narrow = key_own.astype(jnp.bfloat16)
    value_narrow = value_own.astype(jnp.bfloat16)
    normed_grad = (
        against(query_grad, query_all[0])
        + against(key_narrow, key_all[0])
        + against(value_narrow, value_all[0])
    )
    gained = normed_grad * gain_row[None, :]
    head_grad = inverse * gained - trunk_f32 * inverse**3 * jnp.mean(
        trunk_f32 * gained, axis=1, keepdims=True
    )
    result_grad = lax.psum_scatter(head_grad, ("grp", "tp"), scatter_dimension=1, tiled=True)
    return result_grad


def solution(mesh):
    placed = (
        P("ctx", ("grp", "tp")),
        P("grp", "ctx"),
        P("grp", "ctx", "tp"),
        P("grp", "ctx", "tp"),
        P("grp", "ctx", "tp"),
        P("grp", "ctx", "tp"),
    )
    return jax.shard_map(
        body, mesh=mesh, in_specs=placed, out_specs=P("ctx", ("grp", "tp")), check_vma=False
    )
```

profile of v0, /device:TPU:10, one launch (start us, length us, event | category | flops | bytes accessed | tf_op | source)
XLA Modules:
  0.0 592.0 jit_solution(15686336987759858162)
XLA Ops:
  8.8 18.3 %all_gather.22 = bf16[1,4096]{1,0:T(2,128)(2,1)S(1)} all-gather(bf16[1,256]{1,0:T(2,128)(2,1)} %param.11), channel_id=1, replica_groups=mesh['grp'=4,'ctx'=16,'tp'=2] {'ctx'}, dimensions={1}, use_global_device_ids=true | all-gather | bytes 8704 | tf_op jit(solution)/shard_map/all_gather | solution.py:32
  27.1 32.7 %all-gather.7.cloned.1.call-done = bf16[128,4096]{1,0:T(8,128)(2,1)} async-done(((bf16[128,512]{1,0:T(8,128)(2,1)}), bf16[128,4096]{1,0:T(8,128)(2,1)}) %all-gather.7.cloned.1.call-update) | async-done | bytes 1048592 | tf_op jit(solution)/shard_map/all_gather | solution.py:25
  61.3 32.9 %all-gather.15.cloned.1.call-done = bf16[1,4096,256]{2,1,0:T(8,128)(2,1)} async-done(((bf16[1,256,256]{2,1,0:T(8,128)(2,1)}), bf16[1,4096,256]{2,1,0:T(8,128)(2,1)}) %all-gather.15.cloned.1.call-update) | async-done | bytes 2097168 | tf_op jit(solution)/shard_map/all_gather | solution.py:35
  94.3 3.0 fusion.52
  97.4 32.7 %all-gather.9.cloned.1.call-done = bf16[1,4096,256]{2,1,0:T(8,128)(2,1)} async-done(((bf16[1,256,256]{2,1,0:T(8,128)(2,1)}), bf16[1,4096,256]{2,1,0:T(8,128)(2,1)}) %all-gather.9.cloned.1.call-update) | async-done | bytes 2097168 | tf_op jit(solution)/shard_map/all_gather | solution.py:34
  130.1 2.7 fusion.49
  134.5 29.7 %all-gather.17.cloned.1.call-done = bf16[2048,256]{1,0:T(8,128)(2,1)} async-done(((bf16[128,256]{1,0:T(8,128)(2,1)}), bf16[2048,256]{1,0:T(8,128)(2,1)}) %all-gather.17.cloned.1.call-update) | async-done | bytes 1048592 | tf_op jit(solution)/shard_map/all_gather | solution.py:49
  165.7 32.6 %all-gather.11.cloned.1.call-done = bf16[2048,256]{1,0:T(8,128)(2,1)} async-done(((bf16[128,256]{1,0:T(8,128)(2,1)}), bf16[2048,256]{1,0:T(8,128)(2,1)}) %all-gather.11.cloned.1.call-update) | async-done | bytes 1048592 | tf_op jit(solution)/shard_map/all_gather | solution.py:48
  198.3 2.3 copy.33
  200.6 91.0 %all-gather.13.cloned.1.call-done = bf16[1,4096,2048]{2,1,0:T(8,128)(2,1)} async-done(((bf16[1,256,2048]{2,1,0:T(8,128)(2,1)}), bf16[1,4096,2048]{2,1,0:T(8,128)(2,1)}) %all-gather.13.cloned.1.call-update) | async-done | bytes 16777232 | tf_op jit(solution)/shard_map/all_gather | solution.py:33
  291.6 8.2 %fusion.46 = bf16[16,8,16,128]{3,1,2,0:T(8,128)(2,1)S(1)} fusion(bf16[1,4096,2048]{2,1,0:T(8,128)(2,1)} %all-gather.13.cloned.1.call-done, bf16[128,4096]{1,0:T(8,128)(2,1)S(1)} %copy-done, f32[4096]{0:T(1024)S(1)} %bitcast.182, f32[128]{0:T(128)S(1)} %get-tuple-element.269), kind=kOutput, calls=%fused_computation.66 | convolution fusion | flops 2149842944 | bytes 18366976 | tf_op jit(solution)/shard_map/dot_general | solution.py:39
  303.4 16.4 %while.30 = (s32[]{:T(128)}, f32[2,8,128]{2,1,0:T(8,128)S(1)}, f32[2,8,128]{2,1,0:T(8,128)S(1)}, f32[2,8,128,128]{3,2,1,0:T(8,128)}, s32[]{:T(128)}, /*index=5*/...) while((s32[]{:T(128)}, f32[2,8,128]{2,1,0:T(8,128)S(1)}, ...), condition=%wide.region_4.5_spmd.clone, body=%wide.region_1.4_spmd.clone.sunk | while | flops 1890128512 | bytes 25564400 | solution.py:95
  306.6 4.0 fusion.102
  314.8 4.0 fusion.102
  319.8 3.0 copy.32
  324.3 1.6 broadcast_in_dim.43.clone
  327.5 16.5 %while.31 = (s32[]{:T(128)}, f32[128,2,8,128]{0,3,2,1:T(8,128)S(1)}, f32[2048,256]{0,1:T(8,128)}, f32[2048,256]{0,1:T(8,128)}, s32[]{:T(128)}, /*index=5*/bf16[2...) while((s32[]{:T(128)}, ...), condition=%wide.region_7.8_spmd.clone, body=%wide.region_6.7_spmd.clone.sunk | while | flops 1354039936 | bytes 28275928 | solution.py:131
  345.8 11.7 %fusion.26 = f32[128,4096]{1,0:T(8,128)S(1)} fusion(bf16[128,2048]{0,1:T(8,128)(2,1)} %bitcast.177, bf16[1,4096,2048]{2,1,0:T(8,128)(2,1)} %all-gather.13.cloned.1.call-done), kind=kOutput, calls=%fused_computation.42 | convolution fusion | flops 2147483648 | bytes 19398656 | tf_op jit(solution)/shard_map/dot_general | solution.py:18
  357.5 77.5 %reduce-scatter.4.cloned.1.call-done = f32[128,256]{0,1:T(8,128)} async-done(((f32[2048,256]{0,1:T(8,128)}), f32[128,256]{0,1:T(8,128)}) %reduce-scatter.4.cloned.1.call-update) | async-done | bytes 131088 | tf_op jit(solution)/shard_map/reduce_scatter | solution.py:136
  434.9 3.9 convolution_add_fusion.1
  438.8 61.0 %reduce-scatter.6.cloned.1.call-done = f32[128,256]{0,1:T(8,128)} async-done(((f32[2048,256]{0,1:T(8,128)}), f32[128,256]{0,1:T(8,128)}) %reduce-scatter.6.cloned.1.call-update) | async-done | bytes 131088 | tf_op jit(solution)/shard_map/reduce_scatter | solution.py:137
  499.8 3.2 fusion.39
  503.0 1.9 fusion.38
  504.9 80.6 %reduce-scatter.8.cloned.1.call-done = f32[128,512]{1,0:T(8,128)} async-done(((f32[128,4096]{1,0:T(8,128)}), f32[128,512]{1,0:T(8,128)}) %reduce-scatter.8.cloned.1.call-update) | async-done | bytes 262160 | tf_op jit(solution)/shard_map/reduce_scatter | solution.py:150
  (93 shorter events, 40.0 us)
Async XLA Ops:
  6.5 53.3 %all-gather.7.cloned.1.call-start = ((), (), s32[]{:S(2)}) async-start(), calls=%async_computation.3 | async-start | bytes 1179648 | tf_op jit(solution)/shard_map/all_gather | solution.py:25
  7.3 87.0 %all-gather.15.cloned.1.call-start = ((), (), s32[]{:S(2)}) async-start(), calls=%async_computation.7 | async-start | bytes 2228224 | tf_op jit(solution)/shard_map/all_gather | solution.py:35
  8.0 122.1 %all-gather.9.cloned.1.call-start = ((), (), s32[]{:S(2)}) async-start(), calls=%async_computation.4 | async-start | bytes 2228224 | tf_op jit(solution)/shard_map/all_gather | solution.py:34
  8.7 155.4 %all-gather.17.cloned.1.call-start = ((), (), s32[]{:S(2)}) async-start(), calls=%async_computation.8 | async-start | bytes 1114112 | tf_op jit(solution)/shard_map/all_gather | solution.py:49
  61.3 68.8 %copy-start = (bf16[128,4096]{1,0:T(8,128)(2,1)S(1)}, bf16[128,4096]{1,0:T(8,128)(2,1)}, u32[]{:S(2)}) copy-start(bf16[128,4096]{1,0:T(8,128)(2,1)} %all-gather.7.cloned.1.call-done) | copy-start | bytes 3145732
  97.3 36.1 %copy-start.6 = (bf16[1,128,2048]{2,1,0:T(8,128)(2,1)S(1)}, bf16[1,128,2048]{2,1,0:T(8,128)(2,1)}, u32[]{:S(2)}) copy-start(bf16[1,128,2048]{2,1,0:T(8,128)(2,1)} %param.15) | copy-start | bytes 1572868
  97.3 100.9 %all-gather.11.cloned.1.call-start = ((), (), s32[]{:S(2)}) async-start(), calls=%async_computation.5 | async-start | bytes 1114112 | tf_op jit(solution)/shard_map/all_gather | solution.py:48
  132.8 158.8 %all-gather.13.cloned.1.call-start = ((), (), s32[]{:S(2)}) async-start(), calls=%async_computation.6 | async-start | bytes 17825792 | tf_op jit(solution)/shard_map/all_gather | solution.py:33
  133.4 301.5 %reduce-scatter.4.cloned.1.call-start = ((), (), s32[]{:S(2)}) async-start(), calls=%async_computation.9 | async-start | bytes 2228224 | tf_op jit(solution)/shard_map/reduce_scatter | solution.py:136
  299.9 0.8 copy-start.2
  305.4 1.2 copy-start.3
  310.6 1.0 copy-start.4
  313.6 1.2 copy-start.3
  318.8 1.0 copy-start.4
  319.8 3.0 copy-start.1
  319.8 3.0 copy-start.5
  344.0 155.7 %reduce-scatter.6.cloned.1.call-start = ((), (), s32[]{:S(2)}) async-start(), calls=%async_computation.10 | async-start | bytes 2228224 | tf_op jit(solution)/shard_map/reduce_scatter | solution.py:137
  344.8 240.7 %reduce-scatter.8.cloned.1.call-start = ((), (), s32[]{:S(2)}) async-start(), calls=%async_computation.11 | async-start | bytes 2359296 | tf_op jit(solution)/shard_map/reduce_scatter | solution.py:150
Sparse Core Ops, SparseCore 0:
  9.5 50.2 all-gather.6
  61.5 32.7 all-gather.14
  96.0 34.0 all-gather.8
  131.7 32.4 all-gather.16
  165.7 32.4 all-gather.10
  199.8 91.7 all-gather.12
  344.2 90.7 reduce-scatter.3
  437.3 62.4 reduce-scatter.5
  505.0 80.4 reduce-scatter.7
where the time goes:
time: 593 us; the launch traced here: 592 us
  waiting for transfers between devices  474 us (80%)
  matrix products  52.2 us (9%)
  local copies, waits for them, and re-layouts  25.5 us (4%)
  blocking collectives  18.3 us (3%)
  between operations  13.3 us (2%)
  other arithmetic  8.05 us (1%)
    all_gather x1, waiting for transfers between devices, body(): lax.all_gather(w_query, 'ctx', axis=1, tiled=True)  91 us
    reduce_scatter x1, waiting for transfers between devices, body(): lax.psum_scatter(head_grad, ('grp', 'tp'), scatter_dimension=1, tiled=True)  80.6 us
    reduce_scatter x1, waiting for transfers between devices, body(): lax.psum_scatter(key_terms, 'ctx', scatter_dimension=0, tiled=True)  77.5 us
    reduce_scatter x1, waiting for transfers between devices, body(): lax.psum_scatter(value_terms, 'ctx', scatter_dimension=0, tiled=True)  61 us
    all_gather x1, waiting for transfers between devices, body(): lax.all_gather(value_weight, 'ctx', axis=1, tiled=True)  32.9 us
    all_gather x1, waiting for transfers between devices, body(): lax.all_gather(w_key, 'ctx', axis=1, tiled=True)  32.7 us
    all_gather x1, waiting for transfers between devices, body(): features = lax.all_gather(trunk_out, ('grp', 'tp'), axis=1, tiled=True)  32.7 us
    all_gather x1, waiting for transfers between devices, body(): lax.all_gather(key_local, 'ctx', axis=0, tiled=True)  32.6 us
  transfers between devices with their start and end apart: 9, of which 9 were waited for; matrix products, arithmetic and copies ran while one was open for 5% of the time, Pallas kernels for 0%

commit v1 on v0

v1 whole, which is shorter than its diff:
```python
import jax
import jax.numpy as jnp
from jax import lax
from jax.experimental import pallas as pl
from jax.experimental.pallas import tpu as pltpu
from jax.sharding import PartitionSpec as P

HEAD_SIZE = 128
EPSILON = 1e-05
MASKED_SCORE = -1e30
LOG2E = 1.4426950408889634
MESH = pl.DeviceIdType.MESH
ANY = pl.BlockSpec(memory_space=pl.ANY)
BF16 = jnp.bfloat16
F32 = jnp.float32
ROWS = 512
OUT_COLS = 4096
Q_COLS = 512
W_COLS = 640


class Place:
    def __init__(self):
        self.x = lax.axis_index("grp")
        ctx = lax.axis_index("ctx")
        self.ctx = ctx
        self.zh = lax.axis_index("tp")
        self.y = lax.div(ctx, 4)
        self.j = lax.rem(ctx, 4)
        self.zl = lax.div(self.j, 2)
        self.c = lax.rem(ctx, 2)
        self.z = self.zh * 2 + self.zl
        self.known = {}
        for dc in range(2):
            self.keep(dc=dc)
            self.keep(dzl=1, dc=dc)
        for d in range(1, 4):
            self.keep(dx=d)
            self.keep(dy=d)
            self.keep(dz=d)

    def keep(self, **deltas):
        deltas = {key: value for key, value in deltas.items() if value}
        self.known[tuple(sorted(deltas.items()))] = self.work_out(**deltas)

    def at(self, **deltas):
        deltas = {key: value for key, value in deltas.items() if not isinstance(value, int) or value}
        key = tuple(sorted(deltas.items()))
        return self.known[key] if key in self.known else self.work_out(**deltas)

    def work_out(self, dx=0, dy=0, dzl=0, dc=0, dz=0):
        def moved(value, step, size):
            return value if isinstance(step, int) and step == 0 else lax.rem(value + step, size)

        x, y, c = moved(self.x, dx, 4), moved(self.y, dy, 4), moved(self.c, dc, 2)
        zl, zh = moved(self.zl, dzl, 2), self.zh
        if dz:
            z = moved(self.z, dz, 4)
            zl, zh = lax.rem(z, 2), lax.div(z, 2)
        return {"grp": x, "ctx": y * 4 + zl * 2 + c, "tp": zh}


def greet(place, partners):
    barrier = pltpu.get_barrier_semaphore()
    for partner in partners:
        pl.semaphore_signal(barrier, inc=1, device_id=place.at(**partner), device_id_type=MESH)
    pl.semaphore_wait(barrier, len(partners))


def remote(src, dst, send_sem, recv_sem, device):
    return pltpu.make_async_remote_copy(
        src_ref=src, dst_ref=dst, send_sem=send_sem, recv_sem=recv_sem, device_id=device, device_id_type=MESH
    )


J_OTHERS = [dict(dc=1), dict(dzl=1), dict(dzl=1, dc=1)]
PARTNERS = J_OTHERS + [{axis: d} for axis in ("dx", "dy", "dz") for d in (1, 2, 3)]
GATHER_ROWS = ((0, 96), (96, 32))
SUM_ROWS = ((0, 48), (48, 80))


def mm(a, b, contract):
    return lax.dot_general(a, b, ((contract[:1], contract[1:]), ((), ())), preferred_element_type=F32)


def go(src, dst, send_sem, recv_sem, device):
    remote(src, dst, send_sem, recv_sem, device).start()


def arrived(ref, sem):
    pltpu.make_async_copy(ref, ref, sem).wait()


def lanes(index, width=128):
    return pl.ds(pl.multiple_of(index * width, width), width)


def backward_kernel(
    trunk, gain, wq, wk, wv, grads,
    out,
    wq_in, wk_in, wv_in, g_in, kv_cut, q_cut, g_cut,
    x_all, w_kv, w_q, d_all, inv_ref, gains, gain_rows, normed, q_all, g_all, kv, kt, q_turned, g_turned, g_pair, tiles, tops, dq_ref, dk_ref, dv_ref,
    dkv, core_in, back,
    dot_acc, sums, dots,
    relay_in_0, relay_out_0, near_in_0, last_sum_0, last_out_0, last_in_0,
    relay_in_1, relay_out_1, near_in_1, last_sum_1, last_out_1, last_in_1,
    w_send, w_recv, w_set, x_send, x_recv, x_core, gain_send, gain_recv, gain_set, g_send, g_recv,
    kv_send, kv_recv, core_send, core_recv, back_send, back_recv, local,
    swap_send, swap_recv, near_send, near_recv, last_send, last_recv, dot_send, dot_recv,
):
    relay_in, relay_out, near_in = (relay_in_0, relay_in_1), (relay_out_0, relay_out_1), (near_in_0, near_in_1)
    last_sum, last_out, last_in = (last_sum_0, last_sum_1), (last_out_0, last_out_1), (last_in_0, last_in_1)
    p = Place()
    pairs = ((wk.at[0], wk_in), (wv.at[0], wv_in), (wq.at[0], wq_in), (grads.at[0], g_in))
    loads = [pltpu.make_async_copy(src, dst, local.at[i]) for i, (src, dst) in enumerate(pairs)]
    for load in loads:
        load.start()
    greet(p, PARTNERS)

    def j_of(dzl=0, dc=0):
        return lax.rem(p.zl + dzl, 2) * 2 + lax.rem(p.c + dc, 2)

    below, above, across = [lax.rem(p.y + d, 4) for d in (3, 1, 2)]
    j_others = [(j_of(**other), p.at(**other)) for other in J_OTHERS]

    def w_of(piece):
        return w_q.at[piece - 1] if piece else w_kv

    def w_cut(piece):
        return q_cut.at[piece - 1] if piece else kv_cut

    def w_first(piece):
        cut, ref = w_cut(piece), w_of(piece)
        for j in range(4):
            if piece:
                column = j * Q_COLS + (piece - 1) * 256
                cut[j] = wq_in[:, column : column + 256]
            else:
                cut[j] = (wv_in if j % 2 else wk_in)[:, 128 * (j // 2) : 128 * (j // 2) + 128]
        for i, (j, device) in enumerate(j_others):
            go(cut.at[j], ref.at[p.ctx], w_send.at[piece, i], w_recv.at[piece, p.j], device)
        ref[p.ctx] = cut[p.j]

    def w_part(piece, y, part):
        return w_of(piece).at[pl.ds(4 * y + 2 * part, 2)]

    def w_go(piece, y, part, slot, device):
        ref = w_part(piece, y, part)
        go(ref, ref, w_send.at[piece, slot], w_set.at[piece, y, part], device)

    def w_wait(piece, y, part):
        arrived(w_part(piece, y, part), w_set.at[piece, y, part])

    def w_near(piece):
        j, _ = j_others[0]
        arrived(w_of(piece).at[p.y * 4 + j], w_recv.at[piece, j])
        w_go(piece, p.y, p.zl, 3, p.at(dy=1))
        w_go(piece, p.y, p.zl, 4, p.at(dy=3))

    def w_far(piece):
        for j, _ in j_others[1:]:
            arrived(w_of(piece).at[p.y * 4 + j], w_recv.at[piece, j])
        w_go(piece, p.y, 1 - p.zl, 5, p.at(dy=1))
        w_go(piece, p.y, 1 - p.zl, 6, p.at(dy=3))

    def w_relay(piece):
        w_wait(piece, below, 0)
        w_go(piece, below, 0, 7, p.at(dy=1))
        w_wait(piece, above, 1)
        w_go(piece, above, 1, 8, p.at(dy=3))

    def w_rest(piece):
        w_wait(piece, below, 1)
        w_wait(piece, above, 0)
        w_wait(piece, across, 0)
        w_wait(piece, across, 1)

    def x_a(half, d):
        return lax.rem((p.x if half else p.z) + d, 4)

    def x_b(half, d):
        return lax.rem((p.z if half else p.x) + d, 4)

    def a_device(half, da):
        return p.at(dx=da) if half else p.at(dz=da)

    def b_device(half, db):
        return p.at(dz=db) if half else p.at(dx=db)

    def x_piece(half, x, z):
        return x_all.at[lax.rem(z, 2), p.c, x, lax.div(z, 2), pl.ds(*GATHER_ROWS[half])]

    def x_full(half, b, c):
        if half:
            return x_all.at[lax.rem(b, 2), c, :, lax.div(b, 2), pl.ds(*GATHER_ROWS[1])]
        return x_all.at[:, c, b, :, pl.ds(*GATHER_ROWS[0])]

    def x_at(half, da, db):
        a, b = x_a(half, da), x_b(half, db)
        return (x_piece(1, a, b) if half else x_piece(0, b, a)), x_recv.at[half, a, b]

    def x_go(half, da, db, slot, device, src=None):
        dst, sem = x_at(half, da, db)
        go(dst if src is None else src, dst, x_send.at[half, slot], sem, device)

    def x_first(half):
        own = trunk.at[pl.ds(*GATHER_ROWS[half])]
        for i, d in enumerate((2, 1, 3)):
            x_go(half, 0, 0, i, a_device(half, d), own)
        x_go(half, 0, 0, 3, b_device(half, 1), own)
        x_go(half, 0, 0, 4, b_device(half, 3), own)

    def x_second(half):
        for i, d in enumerate((1, 3, 2)):
            arrived(*x_at(half, d, 0))
            x_go(half, d, 0, 5 + 2 * i, b_device(half, 1))
            x_go(half, d, 0, 6 + 2 * i, b_device(half, 3))

    def x_relay(half):
        for i in range(2):
            arrived(*x_at(half, i, 3))
            x_go(half, i, 3, 11 + 2 * i, b_device(half, 1))
            arrived(*x_at(half, 2 + i, 1))
            x_go(half, 2 + i, 1, 12 + 2 * i, b_device(half, 3))

    def x_to_core(half, d):
        b = x_b(half, d)
        ref = x_full(half, b, p.c)
        go(ref, ref, x_send.at[half, 15 + d], x_core.at[half, b], p.at(dc=1))

    halves = (0, 1)
    for half in halves:
        x_first(half)
    loads[0].wait()
    loads[1].wait()
    w_first(0)
    own_x = x_all.at[p.zl, p.c, p.x, p.zh]
    pltpu.make_async_copy(trunk, own_x, local.at[5]).start()
    gains[p.ctx] = jnp.broadcast_to(gain[...], (16, 256))
    for i, (j, device) in enumerate(j_others):
        go(gains.at[p.ctx], gains.at[p.ctx], gain_send.at[i], gain_recv.at[p.j], device)
    w_near(0)
    for half in halves:
        x_second(half)
    w_far(0)
    loads[2].wait()
    w_first(1)
    pltpu.make_async_copy(own_x, own_x, local.at[5]).wait()
    for half in halves:
        x_to_core(half, 0)
    for half in halves:
        x_relay(half)
    w_near(1)
    for j, _ in j_others:
        arrived(gains.at[p.y * 4 + j], gain_recv.at[j])
    gain_y = gains.at[pl.ds(4 * p.y, 4)]
    for dy in (1, 2, 3):
        go(gain_y, gain_y, gain_send.at[2 + dy], gain_set.at[p.y], p.at(dy=dy))
    w_far(1)
    w_relay(0)
    for half in halves:
        for i in range(2):
            arrived(*x_at(half, 2 + i, 3))
            arrived(*x_at(half, i, 1))
        x_to_core(half, 3)
        x_to_core(half, 1)
    w_first(2)
    for half in halves:
        for i in range(4):
            arrived(*x_at(half, i, 2))
        x_to_core(half, 2)
    loads[3].wait()
    for j in range(4):
        g_cut[j] = g_in[:, Q_COLS * j : Q_COLS * j + Q_COLS]
    for i, (j, device) in enumerate(j_others):
        go(g_cut.at[j], g_all.at[p.j], g_send.at[i], g_recv.at[p.j], device)
    g_all[p.j] = g_cut[p.j]
    w_near(2)
    for d in (1, 2, 3):
        y = lax.rem(p.y + d, 4)
        arrived(gains.at[pl.ds(4 * y, 4)], gain_set.at[y])
    for block in range(8):
        row = jnp.concatenate([gains[2 * block][:1], gains[2 * block + 1][:1]], axis=1)
        gain_rows[block] = jnp.broadcast_to(row.astype(F32), (8, 512))
    w_relay(1)
    for half in halves:
        for b in range(4):
            arrived(x_full(half, b, 1 - p.c), x_core.at[half, b])

    @pl.loop(0, 16)
    def _(step):
        group = lax.div(step, 4)
        rows = pl.ds(pl.multiple_of(lax.rem(step, 4) * 32, 32), 32)
        zl, c = lax.div(group, 2), lax.rem(group, 2)
        total = jnp.zeros((32, 128), F32)
        for block in range(8):
            part = x_all[zl, c, block // 2, block % 2, rows].astype(F32)
            part = part * part
            total = total + ((part[:, :128] + part[:, 128:256]) + (part[:, 256:384] + part[:, 384:]))
        inverse = lax.rsqrt(jnp.sum(total, axis=1, keepdims=True) * (1.0 / OUT_COLS) + EPSILON)
        inverse = jnp.broadcast_to(inverse, (32, 128))
        inv_ref[zl, c, rows] = inverse
        wide = jnp.concatenate([inverse] * 4, axis=1)
        for block in range(8):
            scaled = x_all[zl, c, block // 2, block % 2, rows].astype(F32) * wide
            scaled = scaled.reshape(4, 8, 512) * gain_rows[block][None]
            row = pl.ds(pl.multiple_of(step * 32, 32), 32)
            normed[block, row] = scaled.reshape(32, 512).astype(BF16)

    def project(piece):
        ref, width = w_of(piece), 256 if piece else 128

        def step(block, acc):
            right = ref[pl.ds(8 * block, 8)].reshape(2048, width)
            left = jnp.concatenate([normed[4 * block + i] for i in range(4)], axis=1)
            return acc + jnp.dot(left, right, preferred_element_type=F32)

        return lax.fori_loop(0, 2, step, jnp.zeros((ROWS, width), F32)).astype(BF16)

    def project_heads(piece):
        q = project(piece)
        for i in range(2):
            q_all[2 * piece - 2 + i] = q[:, 128 * i : 128 * i + 128]
            q_turned[2 * piece - 2 + i] = jnp.transpose(q[:, 128 * i : 128 * i + 128])

    w_rest(0)
    kv[p.c, p.y] = project(0)
    own_kv = kv.at[p.c, p.y]
    for dy in (1, 2, 3):
        @pl.when(p.y + dy < 4)
        def _():
            go(own_kv, own_kv, kv_send.at[dy - 1], kv_recv.at[p.c, p.y], p.at(dy=dy))

    go(own_kv, own_kv, kv_send.at[3], kv_recv.at[p.c, p.y], p.at(dc=1))
    w_far(2)
    w_rest(1)
    project_heads(1)
    for dy in (1, 3, 2):
        @pl.when(p.y >= dy)
        def _():
            ref = kv.at[p.c, p.y - dy]
            arrived(ref, kv_recv.at[p.c, p.y - dy])
            go(ref, ref, kv_send.at[3 + dy], kv_recv.at[p.c, p.y - dy], p.at(dc=1))

    for j, _ in j_others:
        arrived(g_all.at[j], g_recv.at[j])
    w_relay(2)
    for dy in (0, 1, 3, 2):
        @pl.when(p.y >= dy)
        def _():
            arrived(kv.at[1 - p.c, p.y - dy], kv_recv.at[1 - p.c, p.y - dy])

    scale = HEAD_SIZE ** -0.5
    factor = scale * LOG2E
    dk_ref[...] = jnp.zeros_like(dk_ref)
    dv_ref[...] = jnp.zeros_like(dv_ref)

    @pl.loop(0, p.y + 1)
    def _(block):
        kt[block] = jnp.transpose(kv[0, block])

    def fold(value, combine):
        parts = [value[8 * i : 8 * i + 8] for i in range(4)]
        return combine(combine(parts[0], parts[1]), combine(parts[2], parts[3]))

    def over(row, count):
        return jnp.broadcast_to(row, (count, ROWS))

    def statistics(head, block, s, t, state, diagonal):
        top, total, delta = state
        tiles[head, 1, block] = t
        parts = [s[32 * i : 32 * i + 32] for i in range(16)]
        if diagonal:
            key = lax.broadcasted_iota(jnp.int32, (32, ROWS), 0)
            row = lax.broadcasted_iota(jnp.int32, (32, ROWS), 1)
            parts = [jnp.where(key <= row - 32 * i, part, MASKED_SCORE) for i, part in enumerate(parts)]
        most = fold(parts[0], jnp.maximum)
        for part in parts[1:]:
            most = jnp.maximum(most, fold(part, jnp.maximum))
        now = jnp.maximum(top, jnp.max(most, axis=0, keepdims=True))
        tops[head, block] = over(now, 8)
        wide = over(now, 32)
        sums = jnp.zeros((8, ROWS), F32)
        deltas = jnp.zeros((8, ROWS), F32)
        for i, part in enumerate(parts):
            e = jnp.exp2((part - wide) * factor)
            tiles[head, 0, block, 32 * i : 32 * i + 32] = e
            sums = sums + fold(e, jnp.add)
            deltas = deltas + fold(e * t[32 * i : 32 * i + 32], jnp.add)
        shrink = jnp.exp2((top - now) * factor)
        total = total * shrink + jnp.sum(sums, axis=0, keepdims=True)
        delta = delta * shrink + jnp.sum(deltas, axis=0, keepdims=True)
        return now, total, delta

    def scores(pair, block, states, diagonal):
        products = []
        for head in range(2):
            s = mm(kv[0, block], q_turned[2 * pair + head], (1, 0))
            products.append((s, mm(kv[1, block], g_turned[head], (1, 0))))
        return tuple(statistics(i, block, *products[i], states[i], diagonal) for i in range(2))

    def lows(head, block, stats):
        top, inverse, delta = stats
        weight = over(jnp.exp2((tops[head, block][:1] - top) * factor) * inverse, 32)
        wide = over(delta, 32)
        probs_low, ds_low = [], []
        for i in range(16):
            chunk = pl.ds(32 * i, 32)
            probs = tiles[head, 0, block, chunk] * weight
            probs_low.append(probs.astype(BF16))
            ds_low.append((probs * (tiles[head, 1, block, chunk] - wide)).astype(BF16))
        return jnp.concatenate(probs_low, axis=0), jnp.concatenate(ds_low, axis=0)

    def pair_grads(pair, block, stats):
        both = [lows(head, block, stats[head]) for head in range(2)]
        for head in range(2):
            dq_ref[head] += mm(kt[block], both[head][1], (1, 0))
        probs = jnp.concatenate([both[0][0], both[1][0]], axis=1)
        ds = jnp.concatenate([both[0][1], both[1][1]], axis=1)
        dv_ref[block] += mm(probs, g_pair[...], (1, 0))
        dk_ref[block] += mm(ds, q_all[pl.ds(2 * pair, 2)].reshape(2 * ROWS, HEAD_SIZE), (1, 0))

    def core_go(block):
        return remote(dkv.at[1 - p.c, block], core_in.at[block], core_send.at[block], core_recv.at[block], p.at(dc=1))

    def back_go(block):
        device = {"grp": p.x, "ctx": block * 4 + p.j, "tp": p.zh}
        return remote(dkv.at[p.c, block], back.at[p.y], back_send.at[block], back_recv.at[p.y], device)

    def to_core(block):
        dkv[0, block] = (dk_ref[block] * scale).astype(BF16)
        dkv[1, block] = dv_ref[block].astype(BF16)
        core_go(block).start()

    def to_rows(block):
        core_go(block).wait_recv()
        dkv[p.c, block] = (dkv[p.c, block].astype(F32) + core_in[block].astype(F32)).astype(BF16)
        back_go(block).start()

    @pl.loop(0, 2)
    def _(pair):
        @pl.when(pair == 1)
        def _():
            w_rest(2)
            project_heads(2)

        for head in range(2):
            g = g_all[:, :, lanes(2 * pair + head)].reshape(ROWS, HEAD_SIZE)
            g_pair[ROWS * head : ROWS * head + ROWS] = g
            g_turned[head] = jnp.transpose(g)
        dq_ref[...] = jnp.zeros_like(dq_ref)
        start = (jnp.full((1, ROWS), MASKED_SCORE, F32), jnp.zeros((1, ROWS), F32), jnp.zeros((1, ROWS), F32))
        states = lax.fori_loop(0, p.y, lambda block, now: scores(pair, block, now, False), (start, start))
        states = scores(pair, p.y, states, True)
        stats = []
        for top, total, delta in states:
            inverse = 1.0 / total
            stats.append((top, inverse, delta * inverse))

        @pl.loop(0, p.y + 1)
        def _(block):
            pair_grads(pair, block, stats)

            @pl.when(pair == 1)
            def _():
                to_core(block)

                @pl.when(block > 0)
                def _():
                    to_rows(block - 1)

        for head in range(2):
            dq = jnp.transpose(dq_ref[head] * scale).astype(BF16)
            d_all[:, :, :, lanes(2 * pair + head + 1)] = dq.reshape(2, 2, 128, HEAD_SIZE)

    core_go(p.y).wait_recv()
    dk_ref[0] = dkv[p.c, p.y].astype(F32) + core_in[p.y].astype(F32)
    for dy in (1, 2, 3):
        @pl.when(p.y + dy < 4)
        def _():
            arrived(back.at[p.y + dy], back_recv.at[p.y + dy])
            dk_ref[0] += back[p.y + dy].astype(F32)
    d_all[:, :, :, :128] = dk_ref[0].astype(BF16).reshape(2, 2, 128, HEAD_SIZE)

    dot_acc[...] = jnp.zeros_like(dot_acc)

    def tile_rows(zl, c, i):
        return pl.ds(pl.multiple_of((zl * 2 + c) * 128 + 32 * i, 32), 32)

    def out_block(x, zh):
        block = x * 2 + zh
        left = d_all[...].reshape(ROWS, W_COLS)
        right = [w_of(piece)[pl.ds(2 * block, 2)].reshape(512, 256 if piece else 128) for piece in range(3)]
        part = mm(left, jnp.concatenate(right, axis=1), (1, 1))
        gain_row = gain_rows[block][None]
        for zl in range(2):
            for c in range(2):
                for i in range(4):
                    rows = slice(32 * i, 32 * i + 32)
                    first = (zl * 2 + c) * 128 + 32 * i
                    piece = (part[first : first + 32].reshape(4, 8, 512) * gain_row).reshape(32, 512)
                    tiles[zh, 0, x, first : first + 32] = piece
                    piece = piece * x_all[zl, c, x, zh, rows].astype(F32)
                    piece = (piece[:, :128] + piece[:, 128:256]) + (piece[:, 256:384] + piece[:, 384:])
                    dot_acc[zl, c, rows] += piece
        for zl in range(2):
            for i in range(4):
                rows = slice(32 * i, 32 * i + 32)
                normed[2 * x + zh, 128 * zl + 32 * i : 128 * zl + 32 * i + 32] = tiles[zh, 0, x, tile_rows(zl, 1 - p.c, i)].astype(BF16)

    def swap_out(x, zh):
        return normed.at[2 * x + zh, pl.ds(0, 256)]

    def swap_in(x, zh):
        return normed.at[2 * x + zh, pl.ds(256, 256)]

    def swap(x, zh):
        return remote(swap_out(x, zh), swap_in(x, zh), swap_send.at[x, zh], swap_recv.at[x, zh], p.at(dc=1))

    def out_blocks(x):
        @pl.loop(0, 2)
        def _(zh):
            out_block(x, zh)
            swap(x, zh).start()

    def add_blocks(x):
        @pl.loop(0, 2)
        def _(zh):
            swap(x, zh).wait_recv()
            for zl in range(2):
                for i in range(4):
                    rows = pl.ds(32 * i, 32)
                    total = tiles[zh, 0, x, tile_rows(zl, p.c, i)] + normed[2 * x + zh, 256 + 128 * zl + 32 * i : 288 + 128 * zl + 32 * i].astype(F32)
                    sums[x, zh, zl, rows] = total.astype(BF16)

    def mine(half, da, part):
        a = x_a(half, da)
        if half:
            return sums.at[a, part, :, pl.ds(*SUM_ROWS[1])]
        return sums.at[pl.ds(2 * part, 2), lax.div(a, 2), lax.rem(a, 2), pl.ds(*SUM_ROWS[0])]

    def near_go(half, way, kind):
        step = 3 if way else 1
        if kind == 0:
            src, dst = mine(half, 2, way), relay_in[half].at[way]
        elif kind == 1:
            src, dst = mine(half, step, 1 - way), near_in[half].at[way, 1 - way]
        else:
            src, dst = relay_out[half].at[way], near_in[half].at[way, way]
        return remote(src, dst, near_send.at[half, way, kind], near_recv.at[half, way, kind], a_device(half, step))

    def relay(half, way):
        near_go(half, way, 0).wait_recv()
        step = 3 if way else 1
        total = mine(half, step, way)[...].astype(F32) + relay_in[half][way].astype(F32)
        relay_out[half][way] = total.astype(BF16)
        near_go(half, way, 2).start()

    def last_go(half, db):
        b = x_b(half, db)
        return remote(
            last_out[half].at[b], last_in[half].at[db - 1], last_send.at[half, db - 1], last_recv.at[half, db - 1],
            b_device(half, db),
        )

    def gather_near(half):
        for way in range(2):
            near_go(half, way, 1).wait_recv()
            near_go(half, way, 2).wait_recv()
        for part in range(2):
            total = mine(half, 0, part)[...].astype(F32)
            for way in range(2):
                total = total + near_in[half][way, part].astype(F32)
            last_sum[half][pl.ds(2 * part, 2)] = total
            last_out[half][pl.ds(2 * part, 2)] = total.astype(BF16)
        for db in (2, 1, 3):
            last_go(half, db).start()

    odd = lax.rem(p.x, 2)
    mate = p.x + 1 - 2 * odd
    far, far_mate = lax.rem(p.x + 2, 4), lax.rem(mate + 2, 4)
    far_part = lax.div(far, 2)

    def near_part(part):
        near_go(0, part, 0).start()
        near_go(0, 1 - part, 1).start()

    out_blocks(far)
    out_blocks(far_mate)
    add_blocks(far)
    near_go(1, 0, 0).start()
    near_go(1, 1, 0).start()
    out_blocks(mate)
    add_blocks(far_mate)
    for value in range(2):
        @pl.when(odd == value)
        def _():
            near_go(1, 1 - value, 1).start()

        @pl.when(far_part == value)
        def _():
            near_part(value)

    out_blocks(p.x)
    add_blocks(mate)
    for value in range(2):
        @pl.when(odd == value)
        def _():
            near_go(1, value, 1).start()

    relay(1, 0)
    relay(1, 1)
    add_blocks(p.x)
    for value in range(2):
        @pl.when(far_part == value)
        def _():
            near_part(1 - value)

    for c in range(2):
        for zl in range(2):
            row = jnp.sum(jnp.transpose(dot_acc[zl, c]), axis=0, keepdims=True)
            dots[0, c, zl] = jnp.broadcast_to(row, (8, 128))

    def dot_go(slot, src, dst, device):
        return remote(src, dst, dot_send.at[slot], dot_recv.at[slot], device)

    first_dot = dot_go(0, dots.at[0, 1 - p.c], dots.at[1, 0], p.at(dc=1))
    first_dot.start()
    relay(0, 0)
    relay(0, 1)
    first_dot.wait_recv()
    for zl in range(2):
        dots[1, 1, zl] = dots[0, p.c, zl] + dots[1, 0, zl]
    z_dots = [
        dot_go(dz, dots.at[1, 1, lax.rem(p.zl + dz, 2)], dots.at[2, lax.div(dz, 2), dz % 2], p.at(dz=dz))
        for dz in (1, 2, 3)
    ]
    for copy in z_dots:
        copy.start()
    gather_near(1)
    for copy in z_dots:
        copy.wait_recv()
    dots[3, 0, 0] = (dots[1, 1, p.zl] + dots[2, 0, 1]) + (dots[2, 1, 0] + dots[2, 1, 1])
    x_dots = [
        dot_go(3 + dx, dots.at[3, 0, 0], dots.at[4, dx // 2, dx % 2], p.at(dx=dx)) for dx in (1, 2, 3)
    ]
    for copy in x_dots:
        copy.start()
    gather_near(0)
    for copy in x_dots:
        copy.wait_recv()
    dot = (dots[3, 0, 0] + dots[4, 0, 1]) + (dots[4, 1, 0] + dots[4, 1, 1])
    dot = jnp.transpose(jnp.broadcast_to(dot[:1], (128, 128)))[:, :1] * (1.0 / OUT_COLS)
    inverse = inv_ref[p.zl, p.c][:, :1]
    slope = inverse * inverse * inverse * dot
    for half in (1, 0):
        for db in (1, 2, 3):
            last_go(half, db).wait_recv()
        b = p.z if half else p.x
        total = last_sum[half][b] + last_in[half][0].astype(F32)
        total = total + (last_in[half][1].astype(F32) + last_in[half][2].astype(F32))
        rows = slice(SUM_ROWS[half][0], sum(SUM_ROWS[half]))
        own = x_all[p.zl, p.c, p.x, p.zh, rows].astype(F32)
        out[rows] = inverse[rows] * total - own * slope[rows]

    for x in range(4):
        for zh in range(2):
            swap(x, zh).wait_send()
    for half in halves:
        for way in range(2):
            for kind in range(3):
                near_go(half, way, kind).wait_send()
        for db in (1, 2, 3):
            last_go(half, db).wait_send()
    for copy in [first_dot] + z_dots + x_dots:
        copy.wait_send()

    for piece in range(3):
        for slot in range(9):
            ref = w_of(piece).at[0] if slot < 3 else w_part(piece, 0, 0)
            remote(ref, ref, w_send.at[piece, slot], w_recv.at[piece, 0], p.at(dc=1)).wait_send()
    for half in halves:
        for slot in range(19):
            ref = x_piece(half, 0, 0) if slot < 15 else x_full(half, 0, 0)
            remote(ref, ref, x_send.at[half, slot], x_core.at[half, 0], p.at(dc=1)).wait_send()
    for slot in range(6):
        ref = gains.at[0] if slot < 3 else gain_y
        remote(ref, ref, gain_send.at[slot], gain_recv.at[0], p.at(dc=1)).wait_send()
    for i in range(3):
        remote(g_all.at[0], g_all.at[0], g_send.at[i], g_recv.at[0], p.at(dc=1)).wait_send()
    for dy in (1, 2, 3):
        @pl.when(p.y + dy < 4)
        def _():
            remote(own_kv, own_kv, kv_send.at[dy - 1], kv_recv.at[p.c, p.y], p.at(dc=1)).wait_send()

    for dy in (0, 1, 2, 3):
        @pl.when(p.y >= dy)
        def _():
            remote(own_kv, own_kv, kv_send.at[3 + dy], kv_recv.at[p.c, p.y], p.at(dc=1)).wait_send()

    @pl.loop(0, p.y)
    def _(block):
        core_go(block).wait_send()
        back_go(block).wait_send()

    core_go(p.y).wait_send()


def body(trunk_out, norm_gain, w_query, w_key, value_weight, context_gradient):
    dma, vmem = pltpu.SemaphoreType.DMA, pltpu.VMEM
    halves = []
    for _, rows in SUM_ROWS:
        halves += [
            vmem((2, 2, rows, 512), BF16),
            vmem((2, 2, rows, 512), BF16),
            vmem((2, 2, 2, rows, 512), BF16),
            vmem((4, rows, 512), F32),
            vmem((4, rows, 512), BF16),
            vmem((3, rows, 512), BF16),
        ]
    return pl.pallas_call(
        backward_kernel,
        out_shape=jax.ShapeDtypeStruct((128, 512), F32),
        in_specs=[ANY, pl.BlockSpec(memory_space=pltpu.VMEM)] + [ANY] * 4,
        out_specs=pl.BlockSpec(memory_space=pltpu.VMEM),
        scratch_shapes=[
            vmem((256, 2048), BF16),
            vmem((256, 256), BF16),
            vmem((256, 256), BF16),
            vmem((128, 2048), BF16),
            vmem((4, 256, 128), BF16),
            vmem((2, 4, 256, 256), BF16),
            vmem((4, 128, Q_COLS), BF16),
            vmem((2, 2, 4, 2, 128, 512), BF16),
            vmem((16, 256, 128), BF16),
            vmem((2, 16, 256, 256), BF16),
            vmem((2, 2, 128, W_COLS), BF16),
            vmem((2, 2, 128, 128), F32),
            vmem((16, 16, 256), BF16),
            vmem((8, 8, 512), F32),
            vmem((8, ROWS, 512), BF16),
            vmem((4, ROWS, HEAD_SIZE), BF16),
            vmem((4, 128, Q_COLS), BF16),
            vmem((2, 4, ROWS, HEAD_SIZE), BF16),
            vmem((4, HEAD_SIZE, ROWS), BF16),
            vmem((4, HEAD_SIZE, ROWS), BF16),
            vmem((2, HEAD_SIZE, ROWS), BF16),
            vmem((2 * ROWS, HEAD_SIZE), BF16),
            vmem((2, 2, 4, ROWS, ROWS), F32),
            vmem((2, 4, 8, ROWS), F32),
            vmem((2, HEAD_SIZE, ROWS), F32),
            vmem((4, ROWS, HEAD_SIZE), F32),
            vmem((4, ROWS, HEAD_SIZE), F32),
            vmem((2, 4, ROWS, HEAD_SIZE), BF16),
            vmem((4, ROWS, HEAD_SIZE), BF16),
            vmem((4, ROWS, HEAD_SIZE), BF16),
            vmem((2, 2, 128, 128), F32),
            vmem((4, 2, 2, 128, 512), BF16),
            vmem((5, 2, 2, 8, 128), F32),
            *halves,
            dma((3, 9)), dma((3, 4)), dma((3, 4, 2)),
            dma((2, 19)), dma((2, 4, 4)), dma((2, 4)),
            dma((6,)), dma((4,)), dma((4,)),
            dma((3,)), dma((4,)),
            dma((7,)), dma((2, 4)),
            dma((4,)), dma((4,)), dma((4,)), dma((4,)),
            dma((8,)),
            dma((4, 2)), dma((4, 2)),
            dma((2, 2, 3)), dma((2, 2, 3)),
            dma((2, 3)), dma((2, 3)),
            dma((7,)), dma((7,)),
        ],
        compiler_params=pltpu.CompilerParams(
            collective_id=0, has_side_effects=True, vmem_limit_bytes=60 * 1024 * 1024
        ),
        name="attention_block_backward",
    )(trunk_out, norm_gain, w_query, w_key, value_weight, context_gradient)


def solution(mesh):
    placed = (
        P("ctx", ("grp", "tp")),
        P("grp", "ctx"),
        P("grp", "ctx", "tp"),
        P("grp", "ctx", "tp"),
        P("grp", "ctx", "tp"),
        P("grp", "ctx", "tp"),
    )
    return jax.shard_map(
        body, mesh=mesh, in_specs=placed, out_specs=P("ctx", ("grp", "tp")), check_vma=False
    )
```

time: 593 us -> 112 us (0.19)
  waiting for transfers between devices: 474 us -> 0 us
  Pallas kernels: 0 us -> 108 us
  matrix products: 52.2 us -> 0 us
  local copies, waits for them, and re-layouts: 25.5 us -> 1.67 us
  blocking collectives: 18.3 us -> 0 us
  between operations: 13.3 us -> 0.01 us
  other arithmetic: 8.05 us -> 0 us
    all_gather x6 -> x0, waiting for transfers between devices: 252 us -> none  [the longest x1 91 us: body(): lax.all_gather(w_query, 'ctx', axis=1, tiled=True)]
    reduce_scatter x3 -> x0, waiting for transfers between devices: 219 us -> none  [the longest x1 80.6 us: body(): lax.psum_scatter(head_grad, ('grp', 'tp'), scatter_dimension=1, tiled=True)]
    pallas_call x0 -> x1, Pallas kernels: none -> 108 us  [body(): pl.pallas_call(backward_kernel, out_shape=jax.ShapeDtypeStruct((128, 512)...]
    dot_general x20 -> x0, matrix products: 52.2 us -> none  [the longest x3 18.7 us: against(): lax.dot_general(left_rows, weight_rows, (((1,), (1,)), ((), ())), preferr...]
    all_gather x1 -> x0, blocking collectives: 18.3 us -> none  [body(): lax.all_gather(norm_gain, 'ctx', axis=1, tiled=True)]
  transfers between devices with their start and end apart: 9 -> 0, of which waited for: 9 -> 0; matrix products, arithmetic and copies ran while one was open for 5% -> 0% of each run, Pallas kernels for 0% -> 0%
where the time goes in v1:
time: 112 us; the launch traced here: 110 us
  Pallas kernels  108 us (96%)
  local copies, waits for them, and re-layouts  1.67 us (1%)
    pallas_call x1, Pallas kernels, body(): pl.pallas_call(backward_kernel, out_shape=jax.ShapeDtypeStruct((128, 512)...  108 us

profile of v1, /device:TPU:10, one launch (start us, length us, event | category | flops | bytes accessed | tf_op | source)
XLA Modules:
  0.0 110.0 jit_solution(6629500151314795048)
XLA Ops:
  0.0 108.4 %attention_block_backward.1 = f32[128,512]{1,0:T(8,128)} custom-call(bf16[128,512]{1,0:T(8,128)(2,1)} %trunk.1, bf16[1,256]{1,0:T(2,128)(2,1)} %gain.1, bf16[1,256,2048]{2,1,0:T(8,128)(2,1)} %wq.1, bf16[1,256,256]{2,1,0:T(8,128)(2,1)} %wk.1, bf16[1,256,256]{2,1,0:T(8,128)(2,1)} %wv.1, bf16[1,128,2048]{2,1,0:T(8,128)(2,1)} %grads.1), custom_call_target="tpu_custom_call" | custom-call | tf_op jit(solution)/shard_map/attention_block_backward/pallas_call | solution.py:721
  108.4 1.7 %copy.8 = f32[128,512]{1,0:T(8,128)} copy(f32[128,512]{1,0:T(8,128)} %attention_block_backward.1) | data formatting | bytes 524288

commit v2 on v1

--- a/solution.py
+++ b/solution.py
@@ -76,7 +76,7 @@
 J_OTHERS = [dict(dc=1), dict(dzl=1), dict(dzl=1, dc=1)]
 PARTNERS = J_OTHERS + [{axis: d} for axis in ("dx", "dy", "dz") for d in (1, 2, 3)]
 GATHER_ROWS = ((0, 96), (96, 32))
-SUM_ROWS = ((0, 48), (48, 80))
+SUM_FEATURES = ((0, 192), (192, 320))
 
 
 def mm(a, b, contract):
@@ -99,9 +99,9 @@
     trunk, gain, wq, wk, wv, grads,
     out,
     wq_in, wk_in, wv_in, g_in, kv_cut, q_cut, g_cut,
-    x_all, w_kv, w_q, d_all, inv_ref, gains, gain_rows, normed, q_all, g_all, kv, kt, q_turned, g_turned, g_pair, tiles, tops, dq_ref, dk_ref, dv_ref,
+    x_all, w_kv, w_q, d_turned, inv_ref, inv_rows, own_turned, gains, gain_rows, normed, q_all, g_all, kv, kt, q_turned, g_turned, g_pair, tiles, tops, dq_ref, dk_ref, dv_ref,
     dkv, core_in, back,
-    dot_acc, sums, dots,
+    sums, dots,
     relay_in_0, relay_out_0, near_in_0, last_sum_0, last_out_0, last_in_0,
     relay_in_1, relay_out_1, near_in_1, last_sum_1, last_out_1, last_in_1,
     w_send, w_recv, w_set, x_send, x_recv, x_core, gain_send, gain_recv, gain_set, g_send, g_recv,
@@ -129,7 +129,7 @@
     def w_cut(piece):
         return q_cut.at[piece - 1] if piece else kv_cut
 
-    def w_first(piece):
+    def w_stage(piece):
         cut, ref = w_cut(piece), w_of(piece)
         for j in range(4):
             if piece:
@@ -137,9 +137,13 @@
                 cut[j] = wq_in[:, column : column + 256]
             else:
                 cut[j] = (wv_in if j % 2 else wk_in)[:, 128 * (j // 2) : 128 * (j // 2) + 128]
-        for i, (j, device) in enumerate(j_others):
+        ref[p.ctx] = cut[p.j]
+
+    def w_leave(piece, partners=(0, 1, 2)):
+        cut, ref = w_cut(piece), w_of(piece)
+        for i in partners:
+            j, device = j_others[i]
             go(cut.at[j], ref.at[p.ctx], w_send.at[piece, i], w_recv.at[piece, p.j], device)
-        ref[p.ctx] = cut[p.j]
 
     def w_part(piece, y, part):
         return w_of(piece).at[pl.ds(4 * y + 2 * part, 2)]
@@ -168,12 +172,6 @@
         w_go(piece, below, 0, 7, p.at(dy=1))
         w_wait(piece, above, 1)
         w_go(piece, above, 1, 8, p.at(dy=3))
-
-    def w_rest(piece):
-        w_wait(piece, below, 1)
-        w_wait(piece, above, 0)
-        w_wait(piece, across, 0)
-        w_wait(piece, across, 1)
 
     def x_a(half, d):
         return lax.rem((p.x if half else p.z) + d, 4)
@@ -233,24 +231,28 @@
         x_first(half)
     loads[0].wait()
     loads[1].wait()
-    w_first(0)
+    w_stage(0)
+    w_leave(0)
     own_x = x_all.at[p.zl, p.c, p.x, p.zh]
     pltpu.make_async_copy(trunk, own_x, local.at[5]).start()
     gains[p.ctx] = jnp.broadcast_to(gain[...], (16, 256))
     for i, (j, device) in enumerate(j_others):
         go(gains.at[p.ctx], gains.at[p.ctx], gain_send.at[i], gain_recv.at[p.j], device)
+    loads[2].wait()
+    w_stage(1)
+    w_stage(2)
+    w_leave(1, (0,))
     w_near(0)
+    w_near(1)
     for half in halves:
         x_second(half)
+    w_leave(1, (1, 2))
     w_far(0)
-    loads[2].wait()
-    w_first(1)
     pltpu.make_async_copy(own_x, own_x, local.at[5]).wait()
     for half in halves:
         x_to_core(half, 0)
     for half in halves:
         x_relay(half)
-    w_near(1)
     for j, _ in j_others:
         arrived(gains.at[p.y * 4 + j], gain_recv.at[j])
     gain_y = gains.at[pl.ds(4 * p.y, 4)]
@@ -258,13 +260,14 @@
         go(gain_y, gain_y, gain_send.at[2 + dy], gain_set.at[p.y], p.at(dy=dy))
     w_far(1)
     w_relay(0)
+    own_turned[...] = jnp.transpose(own_x[...].astype(F32))
     for half in halves:
         for i in range(2):
             arrived(*x_at(half, 2 + i, 3))
             arrived(*x_at(half, i, 1))
         x_to_core(half, 3)
         x_to_core(half, 1)
-    w_first(2)
+    w_leave(2)
     for half in halves:
         for i in range(4):
             arrived(*x_at(half, i, 2))
@@ -282,13 +285,19 @@
     for block in range(8):
         row = jnp.concatenate([gains[2 * block][:1], gains[2 * block + 1][:1]], axis=1)
         gain_rows[block] = jnp.broadcast_to(row.astype(F32), (8, 512))
-    w_relay(1)
+    gain_columns = wq_in
+
+    @pl.loop(0, 8)
+    def _(block):
+        turned = jnp.transpose(jnp.broadcast_to(gain_rows[block][:1], (128, 512))).astype(BF16)
+        gain_columns[:, lanes(2 * block)] = turned[:256]
+        gain_columns[:, lanes(2 * block + 1)] = turned[256:]
+
     for half in halves:
         for b in range(4):
             arrived(x_full(half, b, 1 - p.c), x_core.at[half, b])
 
-    @pl.loop(0, 16)
-    def _(step):
+    def norm_rows(step):
         group = lax.div(step, 4)
         rows = pl.ds(pl.multiple_of(lax.rem(step, 4) * 32, 32), 32)
         zl, c = lax.div(group, 2), lax.rem(group, 2)
@@ -310,12 +319,18 @@
     def project(piece):
         ref, width = w_of(piece), 256 if piece else 128
 
-        def step(block, acc):
-            right = ref[pl.ds(8 * block, 8)].reshape(2048, width)
-            left = jnp.concatenate([normed[4 * block + i] for i in range(4)], axis=1)
-            return acc + jnp.dot(left, right, preferred_element_type=F32)
-
-        return lax.fori_loop(0, 2, step, jnp.zeros((ROWS, width), F32)).astype(BF16)
+        def part(y):
+            left = jnp.concatenate([normed[2 * y], normed[2 * y + 1]], axis=1)
+            return jnp.dot(left, ref[pl.ds(4 * y, 4)].reshape(1024, width), preferred_element_type=F32)
+
+        total = part(p.y)
+        w_wait(piece, below, 1)
+        total = total + part(below)
+        w_wait(piece, above, 0)
+        total = total + part(above)
+        w_wait(piece, across, 0)
+        w_wait(piece, across, 1)
+        return (total + part(across)).astype(BF16)
 
     def project_heads(piece):
         q = project(piece)
@@ -323,7 +338,16 @@
             q_all[2 * piece - 2 + i] = q[:, 128 * i : 128 * i + 128]
             q_turned[2 * piece - 2 + i] = jnp.transpose(q[:, 128 * i : 128 * i + 128])
 
-    w_rest(0)
+    @pl.loop(0, 8)
+    def _(step):
+        norm_rows(step)
+
+    w_relay(1)
+
+    @pl.loop(8, 16)
+    def _(step):
+        norm_rows(step)
+
     kv[p.c, p.y] = project(0)
     own_kv = kv.at[p.c, p.y]
     for dy in (1, 2, 3):
@@ -333,7 +357,9 @@
 
     go(own_kv, own_kv, kv_send.at[3], kv_recv.at[p.c, p.y], p.at(dc=1))
     w_far(2)
-    w_rest(1)
+    for zl in range(2):
+        for c in range(2):
+            inv_rows[zl, c] = jnp.transpose(inv_ref[zl, c])[:8]
     project_heads(1)
     for dy in (1, 3, 2):
         @pl.when(p.y >= dy)
@@ -344,7 +370,6 @@
 
     for j, _ in j_others:
         arrived(g_all.at[j], g_recv.at[j])
-    w_relay(2)
     for dy in (0, 1, 3, 2):
         @pl.when(p.y >= dy)
         def _():
@@ -441,7 +466,6 @@
     def _(pair):
         @pl.when(pair == 1)
         def _():
-            w_rest(2)
             project_heads(2)
 
         for head in range(2):
@@ -452,6 +476,11 @@
         start = (jnp.full((1, ROWS), MASKED_SCORE, F32), jnp.zeros((1, ROWS), F32), jnp.zeros((1, ROWS), F32))
         states = lax.fori_loop(0, p.y, lambda block, now: scores(pair, block, now, False), (start, start))
         states = scores(pair, p.y, states, True)
+
+        @pl.when(pair == 0)
+        def _():
+            w_relay(2)
+
         stats = []
         for top, total, delta in states:
             inverse = 1.0 / total
@@ -470,8 +499,7 @@
                     to_rows(block - 1)
 
         for head in range(2):
-            dq = jnp.transpose(dq_ref[head] * scale).astype(BF16)
-            d_all[:, :, :, lanes(2 * pair + head + 1)] = dq.reshape(2, 2, 128, HEAD_SIZE)
+            d_turned[2 * pair + head + 1] = (dq_ref[head] * scale).astype(BF16)
 
     core_go(p.y).wait_recv()
     dk_ref[0] = dkv[p.c, p.y].astype(F32) + core_in[p.y].astype(F32)
@@ -480,33 +508,39 @@
         def _():
             arrived(back.at[p.y + dy], back_recv.at[p.y + dy])
             dk_ref[0] += back[p.y + dy].astype(F32)
-    d_all[:, :, :, :128] = dk_ref[0].astype(BF16).reshape(2, 2, 128, HEAD_SIZE)
-
-    dot_acc[...] = jnp.zeros_like(dot_acc)
-
-    def tile_rows(zl, c, i):
-        return pl.ds(pl.multiple_of((zl * 2 + c) * 128 + 32 * i, 32), 32)
+    d_turned[0] = jnp.transpose(dk_ref[0]).astype(BF16)
+
+    dot = jnp.zeros((8, ROWS), F32)
+    own_turned_kv = jnp.transpose(kv[p.c, p.y])
+    for i in range(5):
+        for k in range(0, 128, 32):
+            turned = q_turned[i - 1, k : k + 32] if i else own_turned_kv[k : k + 32]
+            dot = dot + fold(d_turned[i, k : k + 32].astype(F32) * turned.astype(F32), jnp.add)
+    dot = jnp.sum(dot, axis=0, keepdims=True)
+    for zl in range(2):
+        for c in range(2):
+            group = zl * 2 + c
+            dots[0, c, zl] = jnp.broadcast_to(dot[:, 128 * group : 128 * group + 128], (8, 128)) / inv_rows[zl, c]
 
     def out_block(x, zh):
         block = x * 2 + zh
-        left = d_all[...].reshape(ROWS, W_COLS)
-        right = [w_of(piece)[pl.ds(2 * block, 2)].reshape(512, 256 if piece else 128) for piece in range(3)]
-        part = mm(left, jnp.concatenate(right, axis=1), (1, 1))
-        gain_row = gain_rows[block][None]
+        left = [w_of(piece)[pl.ds(2 * block, 2)].reshape(512, 256 if piece else 128) for piece in range(3)]
+        part = mm(jnp.concatenate(left, axis=1), d_turned[...].reshape(W_COLS, ROWS), (1, 0))
+        for i in range(16):
+            rows = slice(32 * i, 32 * i + 32)
+            gain_column = gain_columns[32 * (i % 8) : 32 * (i % 8) + 32, lanes(2 * block + i // 8)].astype(F32)
+            tiles[zh, 0, x, rows] = part[rows] * jnp.concatenate([gain_column] * 4, axis=1)
         for zl in range(2):
-            for c in range(2):
-                for i in range(4):
-                    rows = slice(32 * i, 32 * i + 32)
-                    first = (zl * 2 + c) * 128 + 32 * i
-                    piece = (part[first : first + 32].reshape(4, 8, 512) * gain_row).reshape(32, 512)
-                    tiles[zh, 0, x, first : first + 32] = piece
-                    piece = piece * x_all[zl, c, x, zh, rows].astype(F32)
-                    piece = (piece[:, :128] + piece[:, 128:256]) + (piece[:, 256:384] + piece[:, 384:])
-                    dot_acc[zl, c, rows] += piece
-        for zl in range(2):
-            for i in range(4):
-                rows = slice(32 * i, 32 * i + 32)
-                normed[2 * x + zh, 128 * zl + 32 * i : 128 * zl + 32 * i + 32] = tiles[zh, 0, x, tile_rows(zl, 1 - p.c, i)].astype(BF16)
+            for i in range(8):
+                rows = slice(64 * i, 64 * i + 64)
+                normed[block, swap_rows(i), swap_lanes(zl, i)] = tiles[zh, 0, x, rows, lanes(zl * 2 + 1 - p.c)].astype(BF16)
+
+    def swap_rows(i, first=0):
+        return slice(first + 64 * (i % 4), first + 64 * (i % 4) + 64)
+
+    def swap_lanes(zl, i):
+        first = 128 * (2 * zl + i // 4)
+        return slice(first, first + 128)
 
     def swap_out(x, zh):
         return normed.at[2 * x + zh, pl.ds(0, 256)]
@@ -528,16 +562,16 @@
         def _(zh):
             swap(x, zh).wait_recv()
             for zl in range(2):
-                for i in range(4):
-                    rows = pl.ds(32 * i, 32)
-                    total = tiles[zh, 0, x, tile_rows(zl, p.c, i)] + normed[2 * x + zh, 256 + 128 * zl + 32 * i : 288 + 128 * zl + 32 * i].astype(F32)
-                    sums[x, zh, zl, rows] = total.astype(BF16)
+                for i in range(8):
+                    rows = slice(64 * i, 64 * i + 64)
+                    other = normed[2 * x + zh, swap_rows(i, 256), swap_lanes(zl, i)].astype(F32)
+                    sums[x, zh, zl, rows] = (tiles[zh, 0, x, rows, lanes(zl * 2 + p.c)] + other).astype(BF16)
 
     def mine(half, da, part):
         a = x_a(half, da)
         if half:
-            return sums.at[a, part, :, pl.ds(*SUM_ROWS[1])]
-        return sums.at[pl.ds(2 * part, 2), lax.div(a, 2), lax.rem(a, 2), pl.ds(*SUM_ROWS[0])]
+            return sums.at[a, part, :, pl.ds(*SUM_FEATURES[1])]
+        return sums.at[pl.ds(2 * part, 2), lax.div(a, 2), lax.rem(a, 2), pl.ds(*SUM_FEATURES[0])]
 
     def near_go(half, way, kind):
         step = 3 if way else 1
@@ -615,11 +649,6 @@
         @pl.when(far_part == value)
         def _():
             near_part(1 - value)
-
-    for c in range(2):
-        for zl in range(2):
-            row = jnp.sum(jnp.transpose(dot_acc[zl, c]), axis=0, keepdims=True)
-            dots[0, c, zl] = jnp.broadcast_to(row, (8, 128))
 
     def dot_go(slot, src, dst, device):
         return remote(src, dst, dot_send.at[slot], dot_recv.at[slot], device)
@@ -650,18 +679,17 @@
     for copy in x_dots:
         copy.wait_recv()
     dot = (dots[3, 0, 0] + dots[4, 0, 1]) + (dots[4, 1, 0] + dots[4, 1, 1])
-    dot = jnp.transpose(jnp.broadcast_to(dot[:1], (128, 128)))[:, :1] * (1.0 / OUT_COLS)
-    inverse = inv_ref[p.zl, p.c][:, :1]
-    slope = inverse * inverse * inverse * dot
+    inverse = inv_rows[p.zl, p.c][:1]
+    slope = inverse * inverse * inverse * dot[:1] * (1.0 / OUT_COLS)
     for half in (1, 0):
         for db in (1, 2, 3):
             last_go(half, db).wait_recv()
         b = p.z if half else p.x
         total = last_sum[half][b] + last_in[half][0].astype(F32)
         total = total + (last_in[half][1].astype(F32) + last_in[half][2].astype(F32))
-        rows = slice(SUM_ROWS[half][0], sum(SUM_ROWS[half]))
-        own = x_all[p.zl, p.c, p.x, p.zh, rows].astype(F32)
-        out[rows] = inverse[rows] * total - own * slope[rows]
+        rows = slice(SUM_FEATURES[half][0], sum(SUM_FEATURES[half]))
+        own_turned[rows] = inverse * total - own_turned[rows] * slope
+    out[...] = jnp.transpose(own_turned[...])
 
     for x in range(4):
         for zh in range(2):
@@ -709,14 +737,14 @@
 def body(trunk_out, norm_gain, w_query, w_key, value_weight, context_gradient):
     dma, vmem = pltpu.SemaphoreType.DMA, pltpu.VMEM
     halves = []
-    for _, rows in SUM_ROWS:
+    for _, rows in SUM_FEATURES:
         halves += [
-            vmem((2, 2, rows, 512), BF16),
-            vmem((2, 2, rows, 512), BF16),
-            vmem((2, 2, 2, rows, 512), BF16),
-            vmem((4, rows, 512), F32),
-            vmem((4, rows, 512), BF16),
-            vmem((3, rows, 512), BF16),
+            vmem((2, 2, rows, 128), BF16),
+            vmem((2, 2, rows, 128), BF16),
+            vmem((2, 2, 2, rows, 128), BF16),
+            vmem((4, rows, 128), F32),
+            vmem((4, rows, 128), BF16),
+            vmem((3, rows, 128), BF16),
         ]
     return pl.pallas_call(
         backward_kernel,
@@ -734,8 +762,10 @@
             vmem((2, 2, 4, 2, 128, 512), BF16),
             vmem((16, 256, 128), BF16),
             vmem((2, 16, 256, 256), BF16),
-            vmem((2, 2, 128, W_COLS), BF16),
+            vmem((5, HEAD_SIZE, ROWS), BF16),
             vmem((2, 2, 128, 128), F32),
+            vmem((2, 2, 8, 128), F32),
+            vmem((512, 128), F32),
             vmem((16, 16, 256), BF16),
             vmem((8, 8, 512), F32),
             vmem((8, ROWS, 512), BF16),
@@ -754,8 +784,7 @@
             vmem((2, 4, ROWS, HEAD_SIZE), BF16),
             vmem((4, ROWS, HEAD_SIZE), BF16),
             vmem((4, ROWS, HEAD_SIZE), BF16),
-            vmem((2, 2, 128, 128), F32),
-            vmem((4, 2, 2, 128, 512), BF16),
+            vmem((4, 2, 2, 512, 128), BF16),
             vmem((5, 2, 2, 8, 128), F32),
             *halves,
             dma((3, 9)), dma((3, 4)), dma((3, 4, 2)),

time: 112 us -> 109 us (0.973)
  Pallas kernels: 108 us -> 106 us
    pallas_call x1, Pallas kernels: 108 us -> 106 us  [body(): pl.pallas_call(backward_kernel, out_shape=jax.ShapeDtypeStruct((128, 512)...]
where the time goes in v2:
time: 109 us; the launch traced here: 107 us
  Pallas kernels  106 us (97%)
  local copies, waits for them, and re-layouts  1.67 us (2%)
    pallas_call x1, Pallas kernels, body(): pl.pallas_call(backward_kernel, out_shape=jax.ShapeDtypeStruct((128, 512)...  106 us

profile of v2, /device:TPU:10, one launch (start us, length us, event | category | flops | bytes accessed | tf_op | source)
XLA Modules:
  0.0 107.3 jit_solution(6211111464354318037)
XLA Ops:
  0.0 105.7 %attention_block_backward.1 = f32[128,512]{1,0:T(8,128)} custom-call(bf16[128,512]{1,0:T(8,128)(2,1)} %trunk.1, bf16[1,256]{1,0:T(2,128)(2,1)} %gain.1, bf16[1,256,2048]{2,1,0:T(8,128)(2,1)} %wq.1, bf16[1,256,256]{2,1,0:T(8,128)(2,1)} %wk.1, bf16[1,256,256]{2,1,0:T(8,128)(2,1)} %wv.1, bf16[1,128,2048]{2,1,0:T(8,128)(2,1)} %grads.1), custom_call_target="tpu_custom_call" | custom-call | tf_op jit(solution)/shard_map/attention_block_backward/pallas_call | solution.py:749
  105.7 1.7 %copy.8 = f32[128,512]{1,0:T(8,128)} copy(f32[128,512]{1,0:T(8,128)} %attention_block_backward.1) | data formatting | bytes 524288

commit v3 on v2

--- a/solution.py
+++ b/solution.py
@@ -278,7 +278,6 @@
     for i, (j, device) in enumerate(j_others):
         go(g_cut.at[j], g_all.at[p.j], g_send.at[i], g_recv.at[p.j], device)
     g_all[p.j] = g_cut[p.j]
-    w_near(2)
     for d in (1, 2, 3):
         y = lax.rem(p.y + d, 4)
         arrived(gains.at[pl.ds(4 * y, 4)], gain_set.at[y])
@@ -293,6 +292,8 @@
         gain_columns[:, lanes(2 * block)] = turned[:256]
         gain_columns[:, lanes(2 * block + 1)] = turned[256:]
 
+    w_relay(1)
+    w_near(2)
     for half in halves:
         for b in range(4):
             arrived(x_full(half, b, 1 - p.c), x_core.at[half, b])
@@ -338,13 +339,7 @@
             q_all[2 * piece - 2 + i] = q[:, 128 * i : 128 * i + 128]
             q_turned[2 * piece - 2 + i] = jnp.transpose(q[:, 128 * i : 128 * i + 128])
 
-    @pl.loop(0, 8)
-    def _(step):
-        norm_rows(step)
-
-    w_relay(1)
-
-    @pl.loop(8, 16)
+    @pl.loop(0, 16)
     def _(step):
         norm_rows(step)
 

time: 109 us -> 110 us (level); the launches traced: 107 us -> 109 us
  Pallas kernels: 106 us -> 108 us
    pallas_call x1, Pallas kernels: 106 us -> 108 us  [body(): pl.pallas_call(backward_kernel, out_shape=jax.ShapeDtypeStruct((128, 512)...]
where the time goes in v3:
time: 110 us; the launch traced here: 109 us
  Pallas kernels  108 us (98%)
  local copies, waits for them, and re-layouts  1.67 us (2%)
    pallas_call x1, Pallas kernels, body(): pl.pallas_call(backward_kernel, out_shape=jax.ShapeDtypeStruct((128, 512)...  108 us

profile of v3, /device:TPU:10, one launch (start us, length us, event | category | flops | bytes accessed | tf_op | source)
XLA Modules:
  0.0 109.5 jit_solution(18250166598788867856)
XLA Ops:
  0.0 107.8 %attention_block_backward.1 = f32[128,512]{1,0:T(8,128)} custom-call(bf16[128,512]{1,0:T(8,128)(2,1)} %trunk.1, bf16[1,256]{1,0:T(2,128)(2,1)} %gain.1, bf16[1,256,2048]{2,1,0:T(8,128)(2,1)} %wq.1, bf16[1,256,256]{2,1,0:T(8,128)(2,1)} %wk.1, bf16[1,256,256]{2,1,0:T(8,128)(2,1)} %wv.1, bf16[1,128,2048]{2,1,0:T(8,128)(2,1)} %grads.1), custom_call_target="tpu_custom_call" | custom-call | tf_op jit(solution)/shard_map/attention_block_backward/pallas_call | solution.py:744
  107.8 1.7 %copy.8 = f32[128,512]{1,0:T(8,128)} copy(f32[128,512]{1,0:T(8,128)} %attention_block_backward.1) | data formatting | bytes 524288

commit v4 on v2

--- a/solution.py
+++ b/solution.py
@@ -241,12 +241,11 @@
     loads[2].wait()
     w_stage(1)
     w_stage(2)
-    w_leave(1, (0,))
+    w_leave(1)
     w_near(0)
     w_near(1)
     for half in halves:
         x_second(half)
-    w_leave(1, (1, 2))
     w_far(0)
     pltpu.make_async_copy(own_x, own_x, local.at[5]).wait()
     for half in halves:

time: 109 us -> 109 us (level); the launches traced: 107 us -> 109 us
  Pallas kernels: 106 us -> 108 us
    pallas_call x1, Pallas kernels: 106 us -> 108 us  [body(): pl.pallas_call(backward_kernel, out_shape=jax.ShapeDtypeStruct((128, 512)...]
where the time goes in v4:
time: 109 us
  Pallas kernels  108 us (99%)
  local copies, waits for them, and re-layouts  1.67 us (2%)
    pallas_call x1, Pallas kernels, body(): pl.pallas_call(backward_kernel, out_shape=jax.ShapeDtypeStruct((128, 512)...  108 us

profile of v4, /device:TPU:10, one launch (start us, length us, event | category | flops | bytes accessed | tf_op | source)
XLA Modules:
  0.0 109.2 jit_solution(6913907413310130154)
XLA Ops:
  0.0 107.5 %attention_block_backward.1 = f32[128,512]{1,0:T(8,128)} custom-call(bf16[128,512]{1,0:T(8,128)(2,1)} %trunk.1, bf16[1,256]{1,0:T(2,128)(2,1)} %gain.1, bf16[1,256,2048]{2,1,0:T(8,128)(2,1)} %wq.1, bf16[1,256,256]{2,1,0:T(8,128)(2,1)} %wk.1, bf16[1,256,256]{2,1,0:T(8,128)(2,1)} %wv.1, bf16[1,128,2048]{2,1,0:T(8,128)(2,1)} %grads.1), custom_call_target="tpu_custom_call" | custom-call | tf_op jit(solution)/shard_map/attention_block_backward/pallas_call | solution.py:748
  107.5 1.7 %copy.8 = f32[128,512]{1,0:T(8,128)} copy(f32[128,512]{1,0:T(8,128)} %attention_block_backward.1) | data formatting | bytes 524288
